TPU v7x, 512 devices: a whole 4x8x8 slice. The times are simulated.
512 devices in a mesh: sib: 2 (over core), row: 16 (over z, y_lo), col: 16 (over x, y_hi).
Axes of the slice: x: 4, y: 8 (y_hi: 4, y_lo: 2; y = y_hi * 2 + y_lo), z: 8, core: 2. Of those that a mesh axis runs over, the one named last changes fastest.
Arguments:
- child_front: float32 [2, 8192, 8192], P('sib', 'row', 'col'), may hold values from -6 to 6
- child_panel: float32 [2, 8192, 1024], P('sib', ('row', 'col')), may hold values from -0.42 to 0.42
- block_map: int32 [2, 64], replicated, may hold values from 0 to 95, as said below
- parent_front: float32 [12288, 12288], P(('row', 'sib'), 'col'), may hold values from -6 to 6
- pivot_inverse: float32 [512, 512], replicated, may hold values from -0.03 to 0.1, as said below
Outputs:
- parent_out: float32 [12288, 12288], P(('row', 'sib'), 'col')
Inputs may be any that keep to these rules, and one draw needn't show every extreme that they name: `block_map`: each row is strictly increasing. A child block i that lands in parent block g * 6 + k with 0 <= k < 6 satisfies g * 4 - 2 <= i < (g + 1) * 4; the lower end is met for g = 1 in every draw, and the last parent block is always named. `pivot_inverse`: lower triangular with diagonal entries from 0.05 to 0.1.
All inputs are finite; a program needn't handle non-finite values.
Results may differ from a plain program's by a relative error of at most 0.0001.
Values sent between devices are 32-bit elements; how exact they have to be, the bound alone decides.
A program may use at most 64 MiB of HBM per device.

v0:
```python
import jax
import jax.numpy as jnp
from jax import lax
from jax.sharding import Mesh
from jax.sharding import PartitionSpec as P

BLK = 128
CBD = 4
PBD = 6
HB = 2
PANEL = 512
ROW = ("row_0", "row_1")
ROW_COL = ("row_0", "row_1", "col")
ROW_SIB = ("row_0", "row_1", "sib")


def broadcast_by_axis(value, axes, root):
    value = jnp.where(lax.axis_index(axes) == root, value, jnp.zeros_like(value))
    for axis in axes:
        value = lax.psum(value, axis)
    return value


def shifted(value, axis, steps):
    count = lax.axis_size(axis)
    initial, last = (max(0, -steps), min(count, count - steps))
    return lax.ppermute(value, axis, [(source, source + steps) for source in range(initial, last)])


def split_up(value, dim, devices):
    shape = value.shape
    blocks = value.reshape(*shape[:dim], devices, shape[dim] // devices, *shape[dim + 1 :])
    return jnp.moveaxis(blocks, dim, 0)


def summed_on_arrival(value, axis, dim):
    blocks = split_up(value, dim, lax.axis_size(axis))
    arrived = lax.all_to_all(blocks, axis, split_axis=0, concat_axis=0, tiled=True)
    return arrived.sum(axis=0)


def padded_to(lines, devices):
    spare = -len(lines) % devices
    return jnp.pad(lines, [(0, spare)] + [(0, 0)] * (lines.ndim - 1))


def spread(value, axis, root):
    lines = jnp.where(lax.axis_index(axis) == root, value, jnp.zeros_like(value)).reshape(
        -1, *value.shape[1:][-1:]
    )
    padded = padded_to(lines, lax.axis_size(axis))
    own = lax.psum_scatter(padded, axis, scatter_dimension=0, tiled=True)
    return lax.all_gather(own, axis, axis=0, tiled=True)[: len(lines)].reshape(value.shape)


def from_everyone(value, axis):
    devices = lax.axis_size(axis)
    return lax.all_to_all(
        jnp.broadcast_to(value[None], (devices, *value.shape)), axis, 0, 0, tiled=True
    )


def joined_along(blocks, dim):
    shape = list(blocks.shape[1:])
    shape[dim] *= blocks.shape[0]
    return jnp.moveaxis(blocks, 0, dim).reshape(shape)


def collect(value, axis, dim):
    blocks = from_everyone(value, axis)
    return joined_along(blocks, dim)


def choose_blocks(block_row, device, child_span, parent_span, edge_span):
    padded = jnp.concatenate([jnp.full((edge_span,), -1, jnp.int32), block_row])
    window = lax.dynamic_slice_in_dim(padded, device * child_span, child_span + edge_span)
    target = device * parent_span + jnp.arange(parent_span, dtype=jnp.int32)
    return (window[None, :] == target[:, None]).astype(jnp.float32)


def times_inverse(rows_part, pivot_inverse):
    return lax.dot_general(
        rows_part,
        pivot_inverse,
        (((1,), (1,)), ((), ())),
        precision=lax.Precision.HIGHEST,
        preferred_element_type=jnp.float32,
    )


def shards(child_front, child_panel, block_map, parent_front, pivot_inverse):
    front_index = lax.axis_index("sib")
    row_index = lax.axis_index(ROW)
    col_index = lax.axis_index("col")
    child_rows = child_front.shape[1]
    parent_rows = parent_front.shape[0]
    parent_cols = parent_front.shape[1]
    edge_width = HB * BLK
    span_blocks = CBD + HB
    rows_local = lax.all_gather(child_panel, "col", axis=1, tiled=True)[0]
    cols_local = broadcast_by_axis(rows_local, ROW, col_index)
    update = child_front[0] - lax.dot_general(
        rows_local,
        cols_local,
        (((1,), (1,)), ((), ())),
        precision=lax.Precision.HIGHEST,
        preferred_element_type=jnp.float32,
    )
    my_map = lax.dynamic_index_in_dim(block_map, front_index, 0, keepdims=False)
    left_cols = shifted(update[:, -edge_width:], "col", 1)
    col_window = jnp.concatenate([left_cols, update], axis=1).reshape(child_rows, span_blocks, BLK)
    col_pick = choose_blocks(my_map, col_index, CBD, PBD, HB)
    spread_cols = jnp.einsum(
        "rwk,qw->rqk", col_window, col_pick, precision=lax.Precision.HIGHEST
    ).reshape(child_rows, PBD * BLK)
    left_rows = shifted(spread_cols[-edge_width:], ROW, 1)
    row_window = jnp.concatenate([left_rows, spread_cols], axis=0).reshape(
        span_blocks, BLK, PBD * BLK
    )
    row_pick = choose_blocks(my_map, row_index, CBD, PBD, HB)
    spread_both = jnp.einsum(
        "wtc,qw->qtc", row_window, row_pick, precision=lax.Precision.HIGHEST
    ).reshape(PBD * BLK, PBD * BLK)
    summed = summed_on_arrival(spread_both, "sib", 0)
    assembled = parent_front + summed
    local_factor = times_inverse(assembled[:, :PANEL], pivot_inverse)
    factor_rows = spread(local_factor, "col", 0)
    owner_rows = broadcast_by_axis(factor_rows, ROW, col_index)
    col_factor = collect(owner_rows, "sib", 0)
    product = lax.dot_general(
        factor_rows,
        col_factor,
        (((1,), (1,)), ((), ())),
        precision=lax.Precision.HIGHEST,
        preferred_element_type=jnp.float32,
    )
    global_rows = (row_index * 2 + front_index) * parent_rows + jnp.arange(
        parent_rows, dtype=jnp.int32
    )
    global_cols = col_index * parent_cols + jnp.arange(parent_cols, dtype=jnp.int32)
    inside = (global_rows[:, None] >= PANEL) & (global_cols[None, :] >= PANEL)
    trailing = jnp.where(inside, assembled - product, assembled)
    factor_wide = jnp.pad(factor_rows, ((0, 0), (0, parent_cols - PANEL)))
    return jnp.where(global_cols[None, :] < PANEL, factor_wide, trailing)


def solution(mesh):
    split = Mesh(
        mesh.devices.reshape(mesh.shape["sib"], 8, 2, mesh.shape["col"]),
        ("sib", "row_0", "row_1", "col"),
    )
    placed = (P("sib", ROW, "col"), P("sib", ROW_COL, None), P(), P(ROW_SIB, "col"), P())
    return jax.shard_map(
        shards, mesh=split, in_specs=placed, out_specs=P(ROW_SIB, "col"), check_vma=False
    )
```

profile of v0, /device:TPU:1, one launch (start us, length us, event | category | flops | bytes accessed | tf_op | source)
XLA Modules:
  0.0 621.0 jit_solution(6062125449259001521)
XLA Ops:
  7.3 72.9 %all-gather.2.cloned.1.call-done = f32[1,512,1024]{2,1,0:T(8,128)} async-done(((f32[1,32,1024]{2,1,0:T(8,128)}), f32[1,512,1024]{2,1,0:T(8,128)}) %all-gather.2.cloned.1.call-update) | async-done | bytes 2097168 | tf_op jit(solution)/shard_map/all_gather | solution.py:100
  80.2 3.2 bitcast_select_fusion
  83.4 82.9 %all-reduce.7.cloned.1.call-done = f32[512,1024]{1,0:T(8,128)} async-done(((f32[512,1024]{1,0:T(8,128)}), f32[512,1024]{1,0:T(8,128)}) %all-reduce.7.cloned.1.call-update) | async-done | bytes 2097168 | tf_op jit(solution)/shard_map/psum | solution.py:20
  166.4 2.7 copy.8
  169.1 81.5 %all-reduce.9.cloned.1.call-done = f32[512,1024]{1,0:T(8,128)} async-done(((f32[512,1024]{1,0:T(8,128)}), f32[512,1024]{1,0:T(8,128)}) %all-reduce.9.cloned.1.call-update) | async-done | bytes 2097168 | tf_op jit(solution)/shard_map/psum | solution.py:20
  250.6 5.4 fusion.8
  256.0 1.0 copy-done.2
  257.0 4.1 collective-permute-start
  261.2 13.7 %collective-permute-done = f32[512,256]{0,1:T(8,128)S(1)} collective-permute-done((f32[512,256]{0,1:T(8,128)S(1)}, f32[512,256]{0,1:T(8,128)S(1)}, u32[]{:S(2)}, u32[]{:S(2)}) %collective-permute-start) | collective-permute-done | bytes 524320 | tf_op jit(solution)/shard_map/ppermute | solution.py:27
  275.0 1.3 pad_maximum_fusion.1
  276.3 1.8 copy.9
  278.2 2.7 convolution_bitcast_fusion
  280.8 1.0 slice.17
  281.9 2.4 copy.10
  284.3 11.1 %collective-permute-start.1 = (f32[256,768]{0,1:T(8,128)}, f32[256,768]{0,1:T(8,128)}, u32[]{:S(2)}, u32[]{:S(2)}) collective-permute-start(f32[256,768]{0,1:T(8,128)} %bitcast.40), channel_id=1, source_target_pairs={{0,16},{16,32},{32,48},{48,64},{64,80},{80,96},{96,112},{112,128},... | collective-permute-start | bytes 2359304 | tf_op jit(solution)/shard_map/ppermute | solution.py:27
  295.4 1.6 copy.11
  297.0 13.2 %collective-permute-done.1 = f32[256,768]{0,1:T(8,128)} collective-permute-done((f32[256,768]{0,1:T(8,128)}, f32[256,768]{0,1:T(8,128)}, u32[]{:S(2)}, u32[]{:S(2)}) %collective-permute-start.1) | collective-permute-done | bytes 786464 | tf_op jit(solution)/shard_map/ppermute | solution.py:27
  310.2 3.2 pad_maximum_fusion
  313.4 2.0 copy.12
  315.4 2.9 fusion
  319.1 7.7 %all_to_all.10 = f32[2,384,768]{2,1,0:T(8,128)S(1)} all-to-all(f32[2,384,768]{2,1,0:T(8,128)S(1)} %bitcast.36), channel_id=1, replica_groups=mesh['sib'=2,'row_0'=8,'row_1'=2,'col'=16] {'sib'}, dimensions={0} | all-to-all | bytes 4718592 | tf_op jit(solution)/shard_map/all_to_all | solution.py:38
  326.8 1.3 reduce_sum.9
  328.0 1.8 add.88
  329.8 2.3 convolution_select_fusion
  332.2 94.5 %reduce-scatter.2.cloned.1.call-done = f32[24,512]{1,0:T(8,128)} async-done(((f32[384,512]{1,0:T(8,128)}), f32[24,512]{1,0:T(8,128)}) %reduce-scatter.2.cloned.1.call-update) | async-done | bytes 49168 | tf_op jit(solution)/shard_map/reduce_scatter | solution.py:52
  426.7 41.6 %all_gather.7 = f32[384,512]{1,0:T(8,128)S(1)} all-gather(f32[24,512]{1,0:T(8,128)} %reduce-scatter.2.cloned.1.call-done), channel_id=1, replica_groups=mesh['sib'=2,'row_0'=8,'row_1'=2,'col'=16] {'col'}, dimensions={0}, use_global_device_ids=true | all-gather | bytes 835584 | tf_op jit(solution)/shard_map/all_gather | solution.py:53
  468.3 0.9 broadcast_select_fusion
  469.3 78.7 %all-reduce.11.cloned.1.call-done = f32[384,512]{1,0:T(8,128)} async-done(((f32[384,512]{1,0:T(8,128)}), f32[384,512]{1,0:T(8,128)}) %all-reduce.11.cloned.1.call-update) | async-done | bytes 786448 | tf_op jit(solution)/shard_map/psum | solution.py:20
  548.1 56.2 %all-reduce.13.cloned.1.call-done = f32[384,512]{1,0:T(8,128)} async-done(((f32[384,512]{1,0:T(8,128)}), f32[384,512]{1,0:T(8,128)}) %all-reduce.13.cloned.1.call-update) | async-done | bytes 786448 | tf_op jit(solution)/shard_map/psum | solution.py:20
  604.3 1.3 broadcast_in_dim.11
  605.6 5.3 all_to_all.11
  610.9 3.2 fusion.4
  (27 shorter events, 1.9 us)
Async XLA Ops:
  6.5 323.3 %copy-start = (f32[512,512]{1,0:T(8,128)S(1)}, f32[512,512]{1,0:T(8,128)}, u32[]{:S(2)}) copy-start(f32[512,512]{1,0:T(8,128)} %param.9) | copy-start | bytes 3145732
  6.5 73.6 %all-gather.2.cloned.1.call-start = ((), (), s32[]{:S(2)}) async-start(), calls=%async_computation.3 | async-start | bytes 2228224 | tf_op jit(solution)/shard_map/all_gather | solution.py:100
  7.3 159.1 %all-reduce.7.cloned.1.call-start = ((), (), s32[]{:S(2)}) async-start(), calls=%async_computation.4 | async-start | bytes 4194304 | tf_op jit(solution)/shard_map/psum | solution.py:20
  83.4 167.2 %all-reduce.9.cloned.1.call-start = ((), (), s32[]{:S(2)}) async-start(), calls=%async_computation.5 | async-start | bytes 4194304 | tf_op jit(solution)/shard_map/psum | solution.py:20
  166.4 84.2 %copy-start.1 = (f32[1,512,1024]{2,1,0:T(8,128)S(1)}, f32[1,512,1024]{2,1,0:T(8,128)}, u32[]{:S(2)}) copy-start(f32[1,512,1024]{2,1,0:T(8,128)} %all-gather.2.cloned.1.call-done) | copy-start | bytes 6291460
  166.4 260.3 %reduce-scatter.2.cloned.1.call-start = ((), (), s32[]{:S(2)}) async-start(), calls=%async_computation.6 | async-start | bytes 835584 | tf_op jit(solution)/shard_map/reduce_scatter | solution.py:52
  169.1 92.0 %copy-start.3 = (s32[2,64]{1,0:T(2,128)S(1)}, s32[2,64]{1,0:T(2,128)}, u32[]{:S(2)}) copy-start(s32[2,64]{1,0:T(2,128)} %param.7) | copy-start | bytes 1540
  256.0 1.0 copy-start.2
  257.0 17.9 %collective-permute-start = (f32[512,256]{0,1:T(8,128)S(1)}, f32[512,256]{0,1:T(8,128)S(1)}, u32[]{:S(2)}, u32[]{:S(2)}) collective-permute-start(f32[512,256]{0,1:T(8,128)S(1)} %slice.16), channel_id=1, source_target_pairs={{0,1},{1,2},{2,3},{3,4},{4,5},{5,6},{6,7},{7,8},{8,9},{9,10},{10,1... | collective-permute-start | bytes 1572872 | tf_op jit(solution)/shard_map/ppermute | solution.py:27
  284.3 25.9 %collective-permute-start.1 = (f32[256,768]{0,1:T(8,128)}, f32[256,768]{0,1:T(8,128)}, u32[]{:S(2)}, u32[]{:S(2)}) collective-permute-start(f32[256,768]{0,1:T(8,128)} %bitcast.40), channel_id=1, source_target_pairs={{0,16},{16,32},{32,48},{48,64},{64,80},{80,96},{96,112},{112,128},... | collective-permute-start | bytes 2359304 | tf_op jit(solution)/shard_map/ppermute | solution.py:27
  332.2 215.8 %all-reduce.11.cloned.1.call-start = ((), (), s32[]{:S(2)}) async-start(), calls=%async_computation.7 | async-start | bytes 1572864 | tf_op jit(solution)/shard_map/psum | solution.py:20
  469.2 135.1 %all-reduce.13.cloned.1.call-start = ((), (), s32[]{:S(2)}) async-start(), calls=%async_computation.8 | async-start | bytes 1572864 | tf_op jit(solution)/shard_map/psum | solution.py:20
Sparse Core Ops, SparseCore 0:
  10.4 69.7 all-gather.1
  83.5 82.8 all-reduce.6
  169.3 81.2 all-reduce.8
  332.3 94.3 reduce-scatter.1
  469.3 78.6 all-reduce.10
  550.7 53.5 all-reduce.12
where the time goes:
time: 621 us
  waiting for transfers between devices  494 us (80%)
  blocking collectives  54.5 us (9%)
  matrix products  16.5 us (3%)
  starting transfers between devices  15.4 us (2%)
  local copies, waits for them, and re-layouts  14.8 us (2%)
  between operations  13.6 us (2%)
  other arithmetic  11.7 us (2%)
    psum x4, waiting for transfers between devices, broadcast_by_axis(): value = lax.psum(value, axis)  299 us
    reduce_scatter x1, waiting for transfers between devices, spread(): own = lax.psum_scatter(padded, axis, scatter_dimension=0, tiled=True)  94.5 us
    all_gather x1, waiting for transfers between devices, shards(): rows_local = lax.all_gather(child_panel, 'col', axis=1, tiled=True)[0]  72.9 us
    all_gather x1, blocking collectives, spread(): lax.all_gather(own, axis, axis=0, tiled=True)[:len(lines)]  41.6 us
    ppermute x2, waiting for transfers between devices, shifted(): lax.ppermute(value, axis, [(source, source + steps) for source in range(i...  26.9 us
    ppermute x2, starting transfers between devices, shifted(): lax.ppermute(value, axis, [(source, source + steps) for source in range(i...  15.2 us
  transfers between devices with their start and end apart: 8, of which 8 were waited for; matrix products, arithmetic and copies ran while one was open for 1% of the time, Pallas kernels for 0%

commit v1 on v0

--- a/solution.py
+++ b/solution.py
@@ -12,6 +12,11 @@
 ROW = ("row_0", "row_1")
 ROW_COL = ("row_0", "row_1", "col")
 ROW_SIB = ("row_0", "row_1", "sib")
+
+
+def all_by_exchange(array, mesh_axis, dim):
+    sent = jnp.stack([array] * lax.axis_size(mesh_axis))
+    return jnp.concatenate(lax.all_to_all(sent, mesh_axis, 0, 0), axis=dim)
 
 
 def broadcast_by_axis(value, axes, root):
@@ -97,7 +102,7 @@
     parent_cols = parent_front.shape[1]
     edge_width = HB * BLK
     span_blocks = CBD + HB
-    rows_local = lax.all_gather(child_panel, "col", axis=1, tiled=True)[0]
+    rows_local = all_by_exchange(child_panel, "col", 1)[0]
     cols_local = broadcast_by_axis(rows_local, ROW, col_index)
     update = child_front[0] - lax.dot_general(
         rows_local,

time: 621 us -> 613 us (0.987)
  waiting for transfers between devices: 494 us -> 475 us
  starting transfers between devices: 15.4 us -> 25.6 us
    all_gather x1 -> x0, waiting for transfers between devices: 72.9 us -> none  [shards(): rows_local = lax.all_gather(child_panel, 'col', axis=1, tiled=True)[0]]
    all_to_all x0 -> x1, waiting for transfers between devices: none -> 49.6 us  [all_by_exchange(): return jnp.concatenate(lax.all_to_all(sent, mesh_axis, 0, 0), axis=dim)]
    all_to_all x0 -> x1, starting transfers between devices: none -> 10.2 us  [all_by_exchange(): return jnp.concatenate(lax.all_to_all(sent, mesh_axis, 0, 0), axis=dim)]
where the time goes in v1:
time: 613 us
  waiting for transfers between devices  475 us (77%)
  blocking collectives  54.5 us (9%)
  starting transfers between devices  25.6 us (4%)
  local copies, waits for them, and re-layouts  17.3 us (3%)
  matrix products  16.5 us (3%)
  between operations  13.3 us (2%)
  other arithmetic  10 us (2%)
    psum x4, waiting for transfers between devices, broadcast_by_axis(): value = lax.psum(value, axis)  304 us
    reduce_scatter x1, waiting for transfers between devices, spread(): own = lax.psum_scatter(padded, axis, scatter_dimension=0, tiled=True)  94.5 us
    all_to_all x1, waiting for transfers between devices, all_by_exchange(): return jnp.concatenate(lax.all_to_all(sent, mesh_axis, 0, 0), axis=dim)  49.6 us
    all_gather x1, blocking collectives, spread(): lax.all_gather(own, axis, axis=0, tiled=True)[:len(lines)]  41.5 us
    ppermute x2, waiting for transfers between devices, shifted(): lax.ppermute(value, axis, [(source, source + steps) for source in range(i...  26.9 us
    ppermute x2, starting transfers between devices, shifted(): lax.ppermute(value, axis, [(source, source + steps) for source in range(i...  15.2 us
  transfers between devices with their start and end apart: 8, of which 8 were waited for; matrix products, arithmetic and copies ran while one was open for 1% of the time, Pallas kernels for 0%

profile of v1, /device:TPU:1, one launch (start us, length us, event | category | flops | bytes accessed | tf_op | source)
XLA Modules:
  0.0 612.5 jit_solution(15379036785573674049)
XLA Ops:
  6.5 2.6 stack.2
  9.1 10.2 %all-to-all-start = ((f32[16,1,32,1024]{3,2,1,0:T(8,128)}), f32[16,1,32,1024]{3,2,1,0:T(8,128)S(1)}, u32[]{:S(2)}, u32[]{:S(2)}) async-start(f32[16,1,32,1024]{3,2,1,0:T(8,128)} %stack.2), calls=%async_computation | async-start | bytes 4194304 | tf_op jit(solution)/shard_map/all_to_all | solution.py:19
  19.4 49.6 %all-to-all-done = f32[16,1,32,1024]{3,2,1,0:T(8,128)S(1)} async-done(((f32[16,1,32,1024]{3,2,1,0:T(8,128)}), f32[16,1,32,1024]{3,2,1,0:T(8,128)S(1)}, u32[]{:S(2)}, u32[]{:S(2)}) %all-to-all-start) | async-done | bytes 2097184 | tf_op jit(solution)/shard_map/all_to_all | solution.py:19
  69.0 1.5 broadcast_select_fusion
  70.6 87.6 %all-reduce.7.cloned.1.call-done = f32[512,1024]{1,0:T(8,128)} async-done(((f32[512,1024]{1,0:T(8,128)}), f32[512,1024]{1,0:T(8,128)}) %all-reduce.7.cloned.1.call-update) | async-done | bytes 2097168 | tf_op jit(solution)/shard_map/psum | solution.py:25
  158.3 2.5 copy.15
  160.8 81.6 %all-reduce.9.cloned.1.call-done = f32[512,1024]{1,0:T(8,128)} async-done(((f32[512,1024]{1,0:T(8,128)}), f32[512,1024]{1,0:T(8,128)}) %all-reduce.9.cloned.1.call-update) | async-done | bytes 2097168 | tf_op jit(solution)/shard_map/psum | solution.py:25
  242.4 5.4 fusion.3
  248.9 4.1 collective-permute-start
  253.1 13.7 %collective-permute-done = f32[512,256]{0,1:T(8,128)S(1)} collective-permute-done((f32[512,256]{0,1:T(8,128)S(1)}, f32[512,256]{0,1:T(8,128)S(1)}, u32[]{:S(2)}, u32[]{:S(2)}) %collective-permute-start) | collective-permute-done | bytes 524320 | tf_op jit(solution)/shard_map/ppermute | solution.py:32
  266.8 1.3 pad_maximum_fusion.1
  268.2 1.9 copy.16
  270.0 2.7 convolution_bitcast_fusion
  272.7 1.0 slice.17
  273.7 2.4 copy.17
  276.1 11.1 %collective-permute-start.1 = (f32[256,768]{0,1:T(8,128)}, f32[256,768]{0,1:T(8,128)}, u32[]{:S(2)}, u32[]{:S(2)}) collective-permute-start(f32[256,768]{0,1:T(8,128)} %bitcast.37), channel_id=1, source_target_pairs={{0,16},{16,32},{32,48},{48,64},{64,80},{80,96},{96,112},{112,128},... | collective-permute-start | bytes 2359304 | tf_op jit(solution)/shard_map/ppermute | solution.py:32
  287.2 1.6 copy.18
  288.9 13.2 %collective-permute-done.1 = f32[256,768]{0,1:T(8,128)} collective-permute-done((f32[256,768]{0,1:T(8,128)}, f32[256,768]{0,1:T(8,128)}, u32[]{:S(2)}, u32[]{:S(2)}) %collective-permute-start.1) | collective-permute-done | bytes 786464 | tf_op jit(solution)/shard_map/ppermute | solution.py:32
  302.0 3.2 pad_maximum_fusion
  305.2 2.0 copy.19
  307.2 2.9 fusion
  310.9 7.7 %all_to_all.15 = f32[2,384,768]{2,1,0:T(8,128)S(1)} all-to-all(f32[2,384,768]{2,1,0:T(8,128)S(1)} %bitcast.33), channel_id=1, replica_groups=mesh['sib'=2,'row_0'=8,'row_1'=2,'col'=16] {'sib'}, dimensions={0} | all-to-all | bytes 4718592 | tf_op jit(solution)/shard_map/all_to_all | solution.py:43
  318.6 1.3 reduce_sum.9
  319.9 1.8 add.88
  321.6 2.3 convolution_select_fusion
  324.1 94.5 %reduce-scatter.2.cloned.1.call-done = f32[24,512]{1,0:T(8,128)} async-done(((f32[384,512]{1,0:T(8,128)}), f32[24,512]{1,0:T(8,128)}) %reduce-scatter.2.cloned.1.call-update) | async-done | bytes 49168 | tf_op jit(solution)/shard_map/reduce_scatter | solution.py:57
  418.5 41.5 %all_gather.3 = f32[384,512]{1,0:T(8,128)S(1)} all-gather(f32[24,512]{1,0:T(8,128)} %reduce-scatter.2.cloned.1.call-done), channel_id=1, replica_groups=mesh['sib'=2,'row_0'=8,'row_1'=2,'col'=16] {'col'}, dimensions={0}, use_global_device_ids=true | all-gather | bytes 835584 | tf_op jit(solution)/shard_map/all_gather | solution.py:58
  461.1 78.8 %all-reduce.11.cloned.1.call-done = f32[384,512]{1,0:T(8,128)} async-done(((f32[384,512]{1,0:T(8,128)}), f32[384,512]{1,0:T(8,128)}) %all-reduce.11.cloned.1.call-update) | async-done | bytes 786448 | tf_op jit(solution)/shard_map/psum | solution.py:25
  539.9 56.2 %all-reduce.13.cloned.1.call-done = f32[384,512]{1,0:T(8,128)} async-done(((f32[384,512]{1,0:T(8,128)}), f32[384,512]{1,0:T(8,128)}) %all-reduce.13.cloned.1.call-update) | async-done | bytes 786448 | tf_op jit(solution)/shard_map/psum | solution.py:25
  596.2 1.3 broadcast_in_dim.11
  597.5 5.3 all_to_all.16
  602.8 3.2 fusion.2
  (25 shorter events, 3.1 us)
Async XLA Ops:
  6.5 315.1 %copy-start = (f32[512,512]{1,0:T(8,128)S(1)}, f32[512,512]{1,0:T(8,128)}, u32[]{:S(2)}) copy-start(f32[512,512]{1,0:T(8,128)} %param.9) | copy-start | bytes 3145732
  9.1 59.9 %all-to-all-start = ((f32[16,1,32,1024]{3,2,1,0:T(8,128)}), f32[16,1,32,1024]{3,2,1,0:T(8,128)S(1)}, u32[]{:S(2)}, u32[]{:S(2)}) async-start(f32[16,1,32,1024]{3,2,1,0:T(8,128)} %stack.2), calls=%async_computation | async-start | bytes 4194304 | tf_op jit(solution)/shard_map/all_to_all | solution.py:19
  19.4 138.9 %all-reduce.7.cloned.1.call-start = ((), (), s32[]{:S(2)}) async-start(), calls=%async_computation.4 | async-start | bytes 4194304 | tf_op jit(solution)/shard_map/psum | solution.py:25
  70.5 171.9 %all-reduce.9.cloned.1.call-start = ((), (), s32[]{:S(2)}) async-start(), calls=%async_computation.5 | async-start | bytes 4194304 | tf_op jit(solution)/shard_map/psum | solution.py:25
  158.2 260.3 %reduce-scatter.2.cloned.1.call-start = ((), (), s32[]{:S(2)}) async-start(), calls=%async_computation.6 | async-start | bytes 835584 | tf_op jit(solution)/shard_map/reduce_scatter | solution.py:57
  242.4 10.5 %copy-start.2 = (s32[2,64]{1,0:T(2,128)S(1)}, s32[2,64]{1,0:T(2,128)}, u32[]{:S(2)}) copy-start(s32[2,64]{1,0:T(2,128)} %param.7) | copy-start | bytes 1540
  247.9 1.0 copy-start.1
  248.9 17.9 %collective-permute-start = (f32[512,256]{0,1:T(8,128)S(1)}, f32[512,256]{0,1:T(8,128)S(1)}, u32[]{:S(2)}, u32[]{:S(2)}) collective-permute-start(f32[512,256]{0,1:T(8,128)S(1)} %slice.16), channel_id=1, source_target_pairs={{0,1},{1,2},{2,3},{3,4},{4,5},{5,6},{6,7},{7,8},{8,9},{9,10},{10,1... | collective-permute-start | bytes 1572872 | tf_op jit(solution)/shard_map/ppermute | solution.py:32
  276.1 25.9 %collective-permute-start.1 = (f32[256,768]{0,1:T(8,128)}, f32[256,768]{0,1:T(8,128)}, u32[]{:S(2)}, u32[]{:S(2)}) collective-permute-start(f32[256,768]{0,1:T(8,128)} %bitcast.37), channel_id=1, source_target_pairs={{0,16},{16,32},{32,48},{48,64},{64,80},{80,96},{96,112},{112,128},... | collective-permute-start | bytes 2359304 | tf_op jit(solution)/shard_map/ppermute | solution.py:32
  324.0 215.9 %all-reduce.11.cloned.1.call-start = ((), (), s32[]{:S(2)}) async-start(), calls=%async_computation.7 | async-start | bytes 1572864 | tf_op jit(solution)/shard_map/psum | solution.py:25
  461.0 135.1 %all-reduce.13.cloned.1.call-start = ((), (), s32[]{:S(2)}) async-start(), calls=%async_computation.8 | async-start | bytes 1572864 | tf_op jit(solution)/shard_map/psum | solution.py:25
Sparse Core Ops, SparseCore 0:
  70.7 87.5 all-reduce.6
  161.1 81.2 all-reduce.8
  324.1 94.3 reduce-scatter.1
  461.1 78.6 all-reduce.10
  542.6 53.5 all-reduce.12
